TPU v7x, 256 devices: a whole 4x4x8 slice. The times are simulated.
256 devices in a mesh: batch: 16 (over y, x), proto: 16 (over z, core).
Axes of the slice: x: 4, y: 4, z: 8, core: 2. Of those that a mesh axis runs over, the one named last changes fastest.
Arguments:
- teacher_emb: bfloat16 [256, 8192], P('proto', 'batch'), may hold values from -22 to 22
- student_emb: bfloat16 [256, 8192], P('proto', 'batch'), may hold values from -6 to 6
- prototypes: bfloat16 [256, 65536], P('batch', 'proto'), may hold values from -16 to 16
Outputs:
- grad_proto: float32 [256, 65536], P('batch', 'proto')
- grad_student: float32 [256, 8192], P('proto', 'batch')
- loss: float32 [], replicated
All inputs are finite; a program needn't handle non-finite values.
Results may differ from a plain program's by a relative error of at most 0.00055.
The roundings to bfloat16 on the way count: a program that leaves them out, or rounds other values in their place, can miss the bound.
Values may be sent and summed in bfloat16 or wider, within the bound.
A program may use at most 64 MiB of HBM per device.

v0:
```python
import jax
import jax.numpy as jnp
from jax import lax
from jax.sharding import PartitionSpec as P

ITERS = 3
teacher_temp = 0.07
student_temp = 0.1
epsilon = 1e-06


def unit(matrix):
    values = matrix.astype(jnp.float32)
    factor = lax.rsqrt(jnp.sum(values * values, axis=0, keepdims=True) + epsilon)
    return ((values * factor).astype(jnp.bfloat16), factor)


def cosine(left, right):
    return lax.dot_general(
        left, right, (((0,), (0,)), ((), ())), preferred_element_type=jnp.float32
    )


def shards(teacher_emb, student_emb, prototypes):
    teacher_full, student_full = (
        lax.all_gather(teacher_emb, "proto", axis=0, tiled=True),
        lax.all_gather(student_emb, "proto", axis=0, tiled=True),
    )
    proto_full = lax.all_gather(prototypes, "batch", axis=0, tiled=True)
    proto_unit, proto_scale = unit(proto_full)
    teacher_unit, unused = unit(teacher_full)
    student_unit, student_scale = unit(student_full)
    width = proto_full.shape[0]
    local_rows = teacher_full.shape[1]
    total_rows = local_rows * lax.axis_size("batch")
    expo = jnp.exp(cosine(teacher_unit, proto_unit) / teacher_temp)
    targets = expo
    for iteration in range(ITERS):
        column_total = lax.psum(jnp.sum(targets, axis=0), "batch")
        targets = targets / column_total[None, :]
        row_total = lax.psum(jnp.sum(targets, axis=1), "proto")
        targets = targets / row_total[:, None]
    cos_student = cosine(student_unit, proto_unit)
    logits = cos_student / student_temp
    partial_total = jnp.sum(jnp.exp(logits), axis=1)
    softmax_total = lax.psum(partial_total, "proto")
    logp = logits - jnp.log(softmax_total)[:, None]
    loss_part = -jnp.sum(targets * logp)
    loss = lax.psum(loss_part, ("batch", "proto")) / total_rows
    grad_logit = ((jnp.exp(logp) - targets) / (total_rows * student_temp)).astype(jnp.bfloat16)
    proto_rows = width // lax.axis_size("batch")
    crop_rows = width // lax.axis_size("proto")
    proto_start = lax.axis_index("batch") * proto_rows
    crop_start = lax.axis_index("proto") * crop_rows
    proto_own = lax.dynamic_slice_in_dim(proto_unit, proto_start, proto_rows, 0).astype(jnp.float32)
    student_own = lax.dynamic_slice_in_dim(student_unit, crop_start, crop_rows, 0).astype(
        jnp.float32
    )
    rows = student_unit
    whole_grad = lax.psum(jnp.dot(rows, grad_logit, preferred_element_type=jnp.float32), "batch")
    proto_part = lax.dynamic_slice_in_dim(whole_grad, proto_start, proto_rows, 0)
    rows = proto_unit
    crop_part = lax.psum_scatter(
        lax.dot_general(
            rows, grad_logit, (((1,), (1,)), ((), ())), preferred_element_type=jnp.float32
        ),
        "proto",
        scatter_dimension=0,
        tiled=True,
    )
    proto_dot = lax.psum(jnp.sum(proto_own * proto_part, axis=0), "batch")
    crop_dot = lax.psum(jnp.sum(student_own * crop_part, axis=0), "proto")
    grad_proto = (proto_part - proto_own * proto_dot[None, :]) * proto_scale
    grad_student = (crop_part - student_own * crop_dot[None, :]) * student_scale
    return (grad_proto, grad_student, loss)


def solution(mesh):
    in_specs = (P("proto", "batch"), P("proto", "batch"), P("batch", "proto"))
    out_specs = (P("batch", "proto"), P("proto", "batch"), P())
    return jax.shard_map(shards, mesh=mesh, in_specs=in_specs, out_specs=out_specs, check_vma=False)
```

profile of v0, /device:TPU:32, one launch (start us, length us, event | category | flops | bytes accessed | tf_op | source)
XLA Modules:
  0.0 646.7 jit_solution(15893222598696431938)
XLA Ops:
  7.2 0.0 all-gather.2.cloned.1.call-start
  7.2 0.7 all-gather.2.cloned.1.call-update
  7.9 0.0 reduce-scatter.2.cloned.1.call-start
  7.9 18.8 %all_gather.11 = bf16[256,512]{1,0:T(8,128)(2,1)S(1)} all-gather(bf16[16,512]{1,0:T(8,128)(2,1)} %param.3), channel_id=1, replica_groups=mesh['batch'=16,'proto'=16] {'proto'}, dimensions={0}, use_global_device_ids=true | all-gather | bytes 278528 | tf_op jit(solution)/shard_map/all_gather | solution.py:26
  26.7 17.3 %all_gather.9 = bf16[256,512]{1,0:T(8,128)(2,1)S(1)} all-gather(bf16[16,512]{1,0:T(8,128)(2,1)} %param.4), channel_id=1, replica_groups=mesh['batch'=16,'proto'=16] {'proto'}, dimensions={0}, use_global_device_ids=true | all-gather | bytes 278528 | tf_op jit(solution)/shard_map/all_gather | solution.py:27
  44.0 0.1 fusion.15
  44.1 0.1 fusion.13
  44.2 18.8 %all-gather.2.cloned.1.call-done = bf16[256,4096]{1,0:T(8,128)(2,1)} async-done(((bf16[16,4096]{1,0:T(8,128)(2,1)}), bf16[256,4096]{1,0:T(8,128)(2,1)}) %all-gather.2.cloned.1.call-update) | async-done | bytes 2097168 | tf_op jit(solution)/shard_map/all_gather | solution.py:29
  63.0 2.0 fusion.11
  65.1 2.1 fusion.12
  67.1 4.7 fusion.25
  71.8 72.1 %psum.78 = f32[4096]{0:T(1024)S(1)} all-reduce(f32[4096]{0:T(1024)S(1)} %get-tuple-element.9), channel_id=1, replica_groups=mesh['batch'=16,'proto'=16] {'batch'}, use_global_device_ids=true, to_apply=%region_6.0 | all-reduce | flops 4096 | bytes 32768 | tf_op jit(solution)/shard_map/psum | solution.py:39
  143.9 4.0 divide_reduce_fusion
  147.9 20.5 %psum.79 = f32[512]{0:T(512)S(1)} all-reduce(f32[512]{0:T(512)S(1)} %divide_reduce_fusion), channel_id=1, replica_groups=mesh['batch'=16,'proto'=16] {'proto'}, use_global_device_ids=true, to_apply=%region_8.0 | all-reduce | flops 512 | bytes 4096 | tf_op jit(solution)/shard_map/psum | solution.py:41
  168.4 4.7 fusion.7
  173.2 69.5 %psum.80 = f32[4096]{0:T(1024)S(1)} all-reduce(f32[4096]{0:T(1024)S(1)} %fusion.7), channel_id=1, replica_groups=mesh['batch'=16,'proto'=16] {'batch'}, use_global_device_ids=true, to_apply=%region_10.0 | all-reduce | flops 4096 | bytes 32768 | tf_op jit(solution)/shard_map/psum | solution.py:39
  242.7 4.3 fusion.8
  247.0 23.5 %psum.81 = f32[512]{0:T(512)S(1)} all-reduce(f32[512]{0:T(512)S(1)} %fusion.8), channel_id=1, replica_groups=mesh['batch'=16,'proto'=16] {'proto'}, use_global_device_ids=true, to_apply=%region_12.0 | all-reduce | flops 512 | bytes 4096 | tf_op jit(solution)/shard_map/psum | solution.py:41
  270.6 4.5 fusion.9
  275.0 69.5 %psum.82 = f32[4096]{0:T(1024)S(1)} all-reduce(f32[4096]{0:T(1024)S(1)} %fusion.9), channel_id=1, replica_groups=mesh['batch'=16,'proto'=16] {'batch'}, use_global_device_ids=true, to_apply=%region_14.0 | all-reduce | flops 4096 | bytes 32768 | tf_op jit(solution)/shard_map/psum | solution.py:39
  344.6 4.6 fusion.10
  349.2 4.6 exponential_reduce_fusion
  353.8 23.7 %all-reduce = (f32[512]{0:T(512)S(1)}, f32[512]{0:T(512)S(1)}) all-reduce(f32[512]{0:T(512)S(1)} %get-tuple-element.7, f32[512]{0:T(512)S(1)} %fusion.10), channel_id=1, replica_groups=mesh['batch'=16,'proto'=16] {'proto'}, use_global_device_ids=true, to_apply=%region_3.0 | all-reduce | flops 1024 | bytes 8192 | tf_op jit(solution)/shard_map/psum | solution.py:46
  377.5 9.5 %multiply_reduce_fusion = (f32[]{:T(128)}, bf16[512,4096]{1,0:T(8,128)(2,1)S(1)}) fusion(f32[512,4096]{1,0:T(8,128)} %get-tuple-element.8, f32[512]{0:T(512)S(1)} %log.3, f32[512,4096]{1,0:T(8,128)} %get-tuple-element.10, f32[512]{0:T(512)S(1)} %get-tuple-element.4, f32[4096]{0:T(1024)S(1)} %psum.82, f32[512]{0:T(512)S(1)} %psum.81, f32[4096]{0:T(1024)S(1)} %psum.80, ...), kind=kLoop, calls=%fused_computation.9 | loop fusion | flops 27262976 | bytes 21028868 | tf_op jit(solution)/shard_map/reduce_sum | solution.py:48
  387.0 0.0 copy-start
  387.0 2.0 copy-done
  389.0 2.1 fusion.27
  391.1 0.0 reduce-scatter.2.cloned.1.call-update
  391.1 0.0 all-reduce.3.cloned.1.call-start
  391.2 5.4 fusion.26
  396.6 0.0 all-reduce.3.cloned.1.call-update
  397.2 78.2 %psum.87 = f32[]{:T(128)} all-reduce(f32[]{:T(128)S(6)} %neg.3), channel_id=1, replica_groups=mesh['batch'=16,'proto'=16] {'batch','proto'}, use_global_device_ids=true, to_apply=%region_24.0 | all-reduce | flops 1 | bytes 8 | tf_op jit(solution)/shard_map/psum | solution.py:49
  476.1 0.0 reduce-scatter.2.cloned.1.call-done
  476.2 0.8 fusion.22
  476.9 22.5 %psum.86 = f32[512]{0:T(512)S(1)} all-reduce(f32[512]{0:T(512)S(1)} %fusion.22), channel_id=1, replica_groups=mesh['batch'=16,'proto'=16] {'proto'}, use_global_device_ids=true, to_apply=%region_22.0 | all-reduce | flops 512 | bytes 4096 | tf_op jit(solution)/shard_map/psum | solution.py:72
  499.4 1.4 fusion.24
  500.8 63.2 %all-reduce.3.cloned.1.call-done = f32[256,4096]{1,0:T(8,128)} async-done(((f32[256,4096]{1,0:T(8,128)}), f32[256,4096]{1,0:T(8,128)}) %all-reduce.3.cloned.1.call-update) | async-done | bytes 4194320 | tf_op jit(solution)/shard_map/psum | solution.py:60
  564.0 1.0 fusion.17
  565.0 72.4 %psum.85 = f32[4096]{0:T(1024)S(1)} all-reduce(f32[4096]{0:T(1024)S(1)} %fusion.17), channel_id=1, replica_groups=mesh['batch'=16,'proto'=16] {'batch'}, use_global_device_ids=true, to_apply=%region_19.0 | all-reduce | flops 4096 | bytes 32768 | tf_op jit(solution)/shard_map/psum | solution.py:71
  637.4 1.7 fusion.19
  (5 shorter events, 0.1 us)
Async XLA Ops:
  7.2 55.8 %all-gather.2.cloned.1.call-start = ((), (), s32[]{:S(2)}) async-start(), calls=%async_computation.1 | async-start | bytes 2228224 | tf_op jit(solution)/shard_map/all_gather | solution.py:29
  7.9 468.3 %reduce-scatter.2.cloned.1.call-start = ((), (), s32[]{:S(2)}) async-start(), calls=%async_computation.3 | async-start | bytes 557056 | tf_op jit(solution)/shard_map/reduce_scatter | solution.py:63
  387.0 2.0 copy-start
  391.1 172.9 %all-reduce.3.cloned.1.call-start = ((), (), s32[]{:S(2)}) async-start(), calls=%async_computation.2 | async-start | bytes 8388608 | tf_op jit(solution)/shard_map/psum | solution.py:60
Sparse Core Ops, SparseCore 0:
  10.4 52.5 all-gather.1
  391.3 53.1 reduce-scatter.1
  448.2 115.7 all-reduce.2
where the time goes:
time: 647 us
  blocking collectives  488 us (75%)
  waiting for transfers between devices  82.7 us (13%)
  other arithmetic  40.8 us (6%)
  matrix products  16.9 us (3%)
  between operations  16.2 us (3%)
    psum x3, blocking collectives, shards(): column_total = lax.psum(jnp.sum(targets, axis=0), 'batch')  211 us
    psum x1, blocking collectives, shards(): loss = lax.psum(loss_part, ('batch', 'proto')) / total_rows  78.2 us
    psum x1, blocking collectives, shards(): proto_dot = lax.psum(jnp.sum(proto_own * proto_part, axis=0), 'batch')  72.4 us
    psum x1, waiting for transfers between devices, shards(): lax.psum(jnp.dot(rows, grad_logit, preferred_element_type=jnp.float32), '...  63.2 us
    psum x2, blocking collectives, shards(): row_total = lax.psum(jnp.sum(targets, axis=1), 'proto')  44.1 us
    psum x1, blocking collectives, shards(): softmax_total = lax.psum(partial_total, 'proto')  23.7 us
    psum x1, blocking collectives, shards(): crop_dot = lax.psum(jnp.sum(student_own * crop_part, axis=0), 'proto')  22.5 us
    all_gather x1, blocking collectives, shards(): lax.all_gather(teacher_emb, 'proto', axis=0, tiled=True)  18.8 us
  transfers between devices with their start and end apart: 3, of which 2 were waited for; matrix products, arithmetic and copies ran while one was open for 1% of the time, Pallas kernels for 0%

commit v1 on v0

--- a/solution.py
+++ b/solution.py
@@ -7,6 +7,27 @@
 teacher_temp = 0.07
 student_temp = 0.1
 epsilon = 1e-06
+
+
+def gather_around(array, axis, dim):
+    size, index, rows = (lax.axis_size(axis), lax.axis_index(axis), array.shape[dim])
+    forward = [(i, (i + 1) % size) for i in range(size)]
+    downward = [(i, (i - 1) % size) for i in range(size)]
+    whole = jnp.zeros((*array.shape[:dim], size * rows, *array.shape[dim + 1 :]), array.dtype)
+    whole = lax.dynamic_update_slice_in_dim(whole, array, index * rows, axis=dim)
+    from_left = from_right = array
+    halfway = size // 2
+    for step in range(1, halfway + 1):
+        from_left = lax.ppermute(from_left, axis, forward)
+        whole = lax.dynamic_update_slice_in_dim(
+            whole, from_left, (index - step) % size * rows, axis=dim
+        )
+        if step < size - halfway:
+            from_right = lax.ppermute(from_right, axis, downward)
+            whole = lax.dynamic_update_slice_in_dim(
+                whole, from_right, (index + step) % size * rows, axis=dim
+            )
+    return whole
 
 
 def unit(matrix):
@@ -23,7 +44,7 @@
 
 def shards(teacher_emb, student_emb, prototypes):
     teacher_full, student_full = (
-        lax.all_gather(teacher_emb, "proto", axis=0, tiled=True),
+        gather_around(teacher_emb, "proto", 0),
         lax.all_gather(student_emb, "proto", axis=0, tiled=True),
     )
     proto_full = lax.all_gather(prototypes, "batch", axis=0, tiled=True)

time: 647 us -> 648 us (level)
  blocking collectives: 488 us -> 472 us
  starting transfers between devices: 0.12 us -> 11.3 us
    all_gather x1 -> x0, blocking collectives: 18.8 us -> none  [shards(): lax.all_gather(teacher_emb, 'proto', axis=0, tiled=True)]
    ppermute x0 -> x15, waiting for transfers between devices: none -> 15.3 us  [the longest x8 8.18 us: gather_around(): from_left = lax.ppermute(from_left, axis, forward)]
    all_gather x1, waiting for transfers between devices: 18.8 us -> 7.44 us  [shards(): proto_full = lax.all_gather(prototypes, 'batch', axis=0, tiled=True)]
    ppermute x0 -> x15, starting transfers between devices: none -> 11.2 us  [the longest x7 10.7 us: gather_around(): from_right = lax.ppermute(from_right, axis, downward)]
  transfers between devices with their start and end apart: 3 -> 18, of which waited for: 2 -> 10; matrix products, arithmetic and copies ran while one was open for 1% -> 1% of each run, Pallas kernels for 0% -> 0%
where the time goes in v1:
time: 648 us; the launch traced here: 647 us
  blocking collectives  472 us (73%)
  waiting for transfers between devices  86.7 us (13%)
  other arithmetic  40.8 us (6%)
  matrix products  16.8 us (3%)
  between operations  16.3 us (3%)
  starting transfers between devices  11.3 us (2%)
    psum x3, blocking collectives, shards(): column_total = lax.psum(jnp.sum(targets, axis=0), 'batch')  211 us
    psum x1, blocking collectives, shards(): loss = lax.psum(loss_part, ('batch', 'proto')) / total_rows  77.3 us
    psum x1, blocking collectives, shards(): proto_dot = lax.psum(jnp.sum(proto_own * proto_part, axis=0), 'batch')  72.4 us
    psum x1, waiting for transfers between devices, shards(): lax.psum(jnp.dot(rows, grad_logit, preferred_element_type=jnp.float32), '...  63.2 us
    psum x2, blocking collectives, shards(): row_total = lax.psum(jnp.sum(targets, axis=1), 'proto')  46 us
    psum x1, blocking collectives, shards(): softmax_total = lax.psum(partial_total, 'proto')  23.7 us
    psum x1, blocking collectives, shards(): crop_dot = lax.psum(jnp.sum(student_own * crop_part, axis=0), 'proto')  21.5 us
    all_gather x1, blocking collectives, shards(): lax.all_gather(student_emb, 'proto', axis=0, tiled=True)  20 us
  transfers between devices with their start and end apart: 18, of which 10 were waited for; matrix products, arithmetic and copies ran while one was open for 1% of the time, Pallas kernels for 0%

profile of v1, /device:TPU:32, one launch (start us, length us, event | category | flops | bytes accessed | tf_op | source)
XLA Modules:
  0.0 646.8 jit_solution(1465383283612602377)
XLA Ops:
  7.2 0.0 all-gather.2.cloned.1.call-start
  7.2 0.7 all-gather.2.cloned.1.call-update
  7.9 0.0 reduce-scatter.2.cloned.1.call-start
  7.9 0.0 collective-permute-start.1
  8.0 0.5 collective-permute-start
  8.5 20.0 %all_gather.6 = bf16[256,512]{1,0:T(8,128)(2,1)S(1)} all-gather(bf16[16,512]{1,0:T(8,128)(2,1)} %param.4), channel_id=1, replica_groups=mesh['batch'=16,'proto'=16] {'proto'}, dimensions={0}, use_global_device_ids=true | all-gather | bytes 278528 | tf_op jit(solution)/shard_map/all_gather | solution.py:48
  28.5 0.1 fusion.13
  28.7 0.7 constant_dynamic-update-slice_fusion.15
  29.4 0.0 collective-permute-done.1
  29.4 0.9 collective-permute-start.3
  30.3 0.0 collective-permute-done
  30.3 0.0 collective-permute-start.2
  30.4 1.4 collective-permute-done.3
  31.8 2.1 collective-permute-start.5
  33.9 0.0 collective-permute-start.4
  33.9 1.4 collective-permute-done.5
  35.4 2.1 collective-permute-start.7
  37.5 0.0 collective-permute-done.4
  37.5 0.0 collective-permute-start.6
  37.5 1.4 collective-permute-done.7
  38.9 1.7 collective-permute-start.9
  40.6 0.0 collective-permute-done.6
  40.6 0.0 collective-permute-start.8
  40.7 1.4 collective-permute-done.9
  42.1 2.0 collective-permute-start.11
  44.1 0.0 collective-permute-done.8
  44.1 1.4 collective-permute-done.11
  45.5 1.7 collective-permute-start.13
  47.3 0.2 collective-permute-done.10
  47.5 4.4 collective-permute-done.12
  51.9 3.6 collective-permute-done.14
  55.5 0.1 fusion.15
  55.6 7.4 %all-gather.2.cloned.1.call-done = bf16[256,4096]{1,0:T(8,128)(2,1)} async-done(((bf16[16,4096]{1,0:T(8,128)(2,1)}), bf16[256,4096]{1,0:T(8,128)(2,1)}) %all-gather.2.cloned.1.call-update) | async-done | bytes 2097168 | tf_op jit(solution)/shard_map/all_gather | solution.py:50
  63.0 2.0 fusion.11
  65.1 2.1 fusion.12
  67.1 4.7 fusion.25
  71.8 72.1 %psum.78 = f32[4096]{0:T(1024)S(1)} all-reduce(f32[4096]{0:T(1024)S(1)} %get-tuple-element.9), channel_id=1, replica_groups=mesh['batch'=16,'proto'=16] {'batch'}, use_global_device_ids=true, to_apply=%region_6.7 | all-reduce | flops 4096 | bytes 32768 | tf_op jit(solution)/shard_map/psum | solution.py:60
  143.9 4.0 divide_reduce_fusion
  147.9 22.5 %psum.79 = f32[512]{0:T(512)S(1)} all-reduce(f32[512]{0:T(512)S(1)} %divide_reduce_fusion), channel_id=1, replica_groups=mesh['batch'=16,'proto'=16] {'proto'}, use_global_device_ids=true, to_apply=%region_8.9 | all-reduce | flops 512 | bytes 4096 | tf_op jit(solution)/shard_map/psum | solution.py:62
  170.4 4.7 fusion.7
  175.1 69.5 %psum.80 = f32[4096]{0:T(1024)S(1)} all-reduce(f32[4096]{0:T(1024)S(1)} %fusion.7), channel_id=1, replica_groups=mesh['batch'=16,'proto'=16] {'batch'}, use_global_device_ids=true, to_apply=%region_10.11 | all-reduce | flops 4096 | bytes 32768 | tf_op jit(solution)/shard_map/psum | solution.py:60
  244.6 4.3 fusion.8
  249.0 23.5 %psum.81 = f32[512]{0:T(512)S(1)} all-reduce(f32[512]{0:T(512)S(1)} %fusion.8), channel_id=1, replica_groups=mesh['batch'=16,'proto'=16] {'proto'}, use_global_device_ids=true, to_apply=%region_12.13 | all-reduce | flops 512 | bytes 4096 | tf_op jit(solution)/shard_map/psum | solution.py:62
  272.5 4.5 fusion.9
  277.0 69.5 %psum.82 = f32[4096]{0:T(1024)S(1)} all-reduce(f32[4096]{0:T(1024)S(1)} %fusion.9), channel_id=1, replica_groups=mesh['batch'=16,'proto'=16] {'batch'}, use_global_device_ids=true, to_apply=%region_14.15 | all-reduce | flops 4096 | bytes 32768 | tf_op jit(solution)/shard_map/psum | solution.py:60
  346.5 4.6 fusion.10
  351.1 4.6 exponential_reduce_fusion
  355.7 23.7 %all-reduce = (f32[512]{0:T(512)S(1)}, f32[512]{0:T(512)S(1)}) all-reduce(f32[512]{0:T(512)S(1)} %get-tuple-element.7, f32[512]{0:T(512)S(1)} %fusion.10), channel_id=1, replica_groups=mesh['batch'=16,'proto'=16] {'proto'}, use_global_device_ids=true, to_apply=%region_3.4 | all-reduce | flops 1024 | bytes 8192 | tf_op jit(solution)/shard_map/psum | solution.py:67
  379.5 9.5 %multiply_reduce_fusion = (f32[]{:T(128)}, bf16[512,4096]{1,0:T(8,128)(2,1)S(1)}) fusion(f32[512,4096]{1,0:T(8,128)} %get-tuple-element.8, f32[512]{0:T(512)S(1)} %log.3, f32[512,4096]{1,0:T(8,128)} %get-tuple-element.10, f32[512]{0:T(512)S(1)} %get-tuple-element.4, f32[4096]{0:T(1024)S(1)} %psum.82, f32[512]{0:T(512)S(1)} %psum.81, f32[4096]{0:T(1024)S(1)} %psum.80, ...), kind=kLoop, calls=%fused_computation.9 | loop fusion | flops 27262976 | bytes 21028868 | tf_op jit(solution)/shard_map/reduce_sum | solution.py:69
  389.0 2.0 copy-done
  390.9 2.1 fusion.27
  393.0 0.0 reduce-scatter.2.cloned.1.call-update
  393.1 0.0 all-reduce.3.cloned.1.call-start
  393.1 5.4 fusion.26
  398.5 0.0 all-reduce.3.cloned.1.call-update
  399.2 77.3 %psum.87 = f32[]{:T(128)} all-reduce(f32[]{:T(128)S(6)} %neg.3), channel_id=1, replica_groups=mesh['batch'=16,'proto'=16] {'batch','proto'}, use_global_device_ids=true, to_apply=%region_24.25 | all-reduce | flops 1 | bytes 8 | tf_op jit(solution)/shard_map/psum | solution.py:70
  477.1 0.0 reduce-scatter.2.cloned.1.call-done
  477.1 0.8 fusion.22
  477.9 21.5 %psum.86 = f32[512]{0:T(512)S(1)} all-reduce(f32[512]{0:T(512)S(1)} %fusion.22), channel_id=1, replica_groups=mesh['batch'=16,'proto'=16] {'proto'}, use_global_device_ids=true, to_apply=%region_22.23 | all-reduce | flops 512 | bytes 4096 | tf_op jit(solution)/shard_map/psum | solution.py:93
  499.4 1.4 fusion.24
  500.8 63.2 %all-reduce.3.cloned.1.call-done = f32[256,4096]{1,0:T(8,128)} async-done(((f32[256,4096]{1,0:T(8,128)}), f32[256,4096]{1,0:T(8,128)}) %all-reduce.3.cloned.1.call-update) | async-done | bytes 4194320 | tf_op jit(solution)/shard_map/psum | solution.py:81
  564.0 1.0 fusion.17
  565.0 72.4 %psum.85 = f32[4096]{0:T(1024)S(1)} all-reduce(f32[4096]{0:T(1024)S(1)} %fusion.17), channel_id=1, replica_groups=mesh['batch'=16,'proto'=16] {'batch'}, use_global_device_ids=true, to_apply=%region_19.20 | all-reduce | flops 4096 | bytes 32768 | tf_op jit(solution)/shard_map/psum | solution.py:92
  637.4 1.7 fusion.19
  (27 shorter events, 0.2 us)
Async XLA Ops:
  7.2 55.8 %all-gather.2.cloned.1.call-start = ((), (), s32[]{:S(2)}) async-start(), calls=%async_computation.1 | async-start | bytes 2228224 | tf_op jit(solution)/shard_map/all_gather | solution.py:50
  7.9 469.2 %reduce-scatter.2.cloned.1.call-start = ((), (), s32[]{:S(2)}) async-start(), calls=%async_computation.3 | async-start | bytes 557056 | tf_op jit(solution)/shard_map/reduce_scatter | solution.py:84
  7.9 21.5 %collective-permute-start.1 = (bf16[16,512]{1,0:T(8,128)(2,1)}, bf16[16,512]{1,0:T(8,128)(2,1)S(1)}, u32[]{:S(2)}, u32[]{:S(2)}) collective-permute-start(bf16[16,512]{1,0:T(8,128)(2,1)} %param.3), channel_id=1, source_target_pairs={{0,15},{1,0},{2,1},{3,2},{4,3},{5,4},{6,5},{7,6},{8,7},{9,8},{10,9... | collective-permute-start | bytes 49160 | tf_op jit(solution)/shard_map/ppermute | solution.py:26
  8.0 22.4 %collective-permute-start = (bf16[16,512]{1,0:T(8,128)(2,1)}, bf16[16,512]{1,0:T(8,128)(2,1)S(1)}, u32[]{:S(2)}, u32[]{:S(2)}) collective-permute-start(bf16[16,512]{1,0:T(8,128)(2,1)} %param.3), channel_id=1, source_target_pairs={{0,1},{1,2},{2,3},{3,4},{4,5},{5,6},{6,7},{7,8},{8,9},{9,10},{10,1... | collective-permute-start | bytes 49160 | tf_op jit(solution)/shard_map/ppermute | solution.py:21
  29.4 2.4 collective-permute-start.3
  30.3 3.6 collective-permute-start.2
  31.8 3.6 collective-permute-start.5
  33.9 3.6 collective-permute-start.4
  35.4 3.6 collective-permute-start.7
  37.5 3.2 collective-permute-start.6
  38.9 3.2 collective-permute-start.9
  40.6 3.5 collective-permute-start.8
  42.1 3.5 collective-permute-start.11
  44.1 3.4 collective-permute-start.10
  45.5 6.3 collective-permute-start.13
  47.5 4.4 collective-permute-start.12
  51.9 3.6 collective-permute-start.14
  388.9 2.0 copy-start
  393.1 171.0 %all-reduce.3.cloned.1.call-start = ((), (), s32[]{:S(2)}) async-start(), calls=%async_computation.2 | async-start | bytes 8388608 | tf_op jit(solution)/shard_map/psum | solution.py:81
Sparse Core Ops, SparseCore 0:
  10.4 52.5 all-gather.1
  393.2 51.1 reduce-scatter.1
  448.1 115.8 all-reduce.2
